TPU v7x, 32 devices: a whole 2x2x4 slice. The times are simulated.
32 devices in a mesh: own: 16 (over z, y, x), rep: 2 (over core).
Axes of the slice: x: 2, y: 2, z: 4, core: 2. Of those that a mesh axis runs over, the one named last changes fastest.
Arguments:
- tokens: bfloat16 [4096, 2560], P(('own', 'rep')), may hold values from -6 to 6
- cotangent: bfloat16 [4096, 2560], P(('own', 'rep')), may hold values from -6 to 6
- route: int32 [4096, 6], P(('own', 'rep')), may hold values from 0 to 159, all different within a row; in each aligned block of 128 rows (0 to 127, 128 to 255, ...) at most 6 rows name the same one
- gate_index: int32 [4096, 6], P(('own', 'rep')), may hold values from 0 to 255
- gate_table: float32 [256], replicated, may hold values from 0.1 to 1
- w_gate: bfloat16 [4096, 2560], P(('own', 'rep')), may hold values from -0.125 to 0.125
- w_up: bfloat16 [4096, 2560], P(('own', 'rep')), may hold values from -0.125 to 0.125
- w_down: bfloat16 [4096, 2560], P(('own', 'rep')), may hold values from -0.1875 to 0.1875
Outputs:
- grad_tokens: bfloat16 [4096, 2560], P(('own', 'rep'))
- grad_w_gate: float32 [4096, 2560], P(('own', 'rep'))
- grad_w_up: float32 [4096, 2560], P(('own', 'rep'))
- grad_w_down: float32 [4096, 2560], P(('own', 'rep'))
Inputs may be any that keep to these rules, and one draw needn't show every extreme that they name: `route`: each row names 6 different experts. Among the rows of one device no expert is named by more than 6 rows, and in some device some expert is named by exactly 6.
All inputs are finite; a program needn't handle non-finite values.
Results may differ from a plain program's by a relative error of at most 0.015.
Values may be sent and summed in bfloat16 or wider, within the bound.
A program may use at most 64 MiB of HBM per device.

v0:
```python
import jax
import jax.numpy as jnp
from jax import lax
from jax.sharding import PartitionSpec as P

SPLIT = 4
CAP = 6


def silu_parts(pre_gate):
    sigmoid_value = jax.nn.sigmoid(pre_gate)
    return (pre_gate * sigmoid_value, sigmoid_value * (1.0 + pre_gate * (1.0 - sigmoid_value)))


def panel_terms(rows_x, rows_cot, panel_gate, panel_up, panel_down):
    pre_gate = jnp.dot(rows_x, panel_gate.T, preferred_element_type=jnp.float32)
    pre_up = jnp.dot(rows_x, panel_up.T, preferred_element_type=jnp.float32)
    active, slope_value = silu_parts(pre_gate)
    hidden = (active * pre_up).astype(jnp.bfloat16)
    hidden_delta = jnp.dot(rows_cot, panel_down.T, preferred_element_type=jnp.float32)
    gate_delta = (hidden_delta * pre_up * slope_value).astype(jnp.bfloat16)
    up_delta = (hidden_delta * active).astype(jnp.bfloat16)
    grad_rows = jnp.dot(gate_delta, panel_gate, preferred_element_type=jnp.float32) + jnp.dot(
        up_delta, panel_up, preferred_element_type=jnp.float32
    )
    grad_gate = jnp.dot(gate_delta.T, rows_x, preferred_element_type=jnp.float32)
    grad_up = jnp.dot(up_delta.T, rows_x, preferred_element_type=jnp.float32)
    grad_down = jnp.dot(hidden.T, rows_cot, preferred_element_type=jnp.float32)
    return (grad_rows, grad_gate, grad_up, grad_down)


def per_device(tokens, cotangent, route, gate_index, gate_table, w_gate, w_up, w_down):
    owners = lax.axis_size("own")
    experts_here = owners // SPLIT
    tok_count = tokens.shape[0]
    model_width = tokens.shape[1]
    choices_each = route.shape[1]
    table_hits = (
        gate_index[:, :, None] == jnp.arange(gate_table.shape[0], dtype=jnp.int32)[None, None, :]
    ).astype(jnp.float32)
    gate_values = jnp.sum(table_hits * gate_table[None, None, :], axis=2).reshape(-1)
    is_named = (
        route.reshape(-1)[:, None] == jnp.arange(experts_here, dtype=jnp.int32)[None, :]
    ).astype(jnp.int32)
    earlier = jnp.cumsum(is_named, axis=0) - is_named
    slot_hits = (
        is_named[:, :, None]
        * (earlier[:, :, None] == jnp.arange(CAP, dtype=jnp.int32)[None, None, :]).astype(jnp.int32)
    ).astype(jnp.float32)
    slot_hits = slot_hits.reshape(tok_count * choices_each, experts_here * CAP)
    select = slot_hits.reshape(tok_count, choices_each, experts_here * CAP).sum(axis=1)
    slot_gate = jnp.dot(
        gate_values, slot_hits, precision=lax.Precision.HIGHEST, preferred_element_type=jnp.float32
    )
    picker = select.astype(jnp.bfloat16)
    sent_x = jnp.dot(picker.T, tokens, preferred_element_type=jnp.float32).astype(jnp.bfloat16)
    sent_dy = jnp.dot(picker.T, cotangent, preferred_element_type=jnp.float32)
    sent_cot = (slot_gate[:, None] * sent_dy).astype(jnp.bfloat16)

    def fan_out(slot_rows):
        spread = jnp.broadcast_to(
            slot_rows.reshape(experts_here, 1, CAP, model_width),
            (experts_here, SPLIT, CAP, model_width),
        )
        return spread.reshape(owners, CAP, model_width)

    got_x, got_cot = (
        lax.all_to_all(fan_out(sent_x), "own", split_axis=0, concat_axis=0, tiled=True),
        lax.all_to_all(fan_out(sent_cot), "own", split_axis=0, concat_axis=0, tiled=True),
    )
    rows_x = got_x.reshape(owners * CAP, model_width)
    rows_cot = got_cot.reshape(owners * CAP, model_width)
    full_gate, full_up, full_down = (
        lax.all_gather(w_gate, "rep", axis=0, tiled=True),
        lax.all_gather(w_up, "rep", axis=0, tiled=True),
        lax.all_gather(w_down, "rep", axis=0, tiled=True),
    )
    grad_rows, grad_gate, grad_up, grad_down = panel_terms(
        rows_x, rows_cot, full_gate, full_up, full_down
    )
    block_rows = grad_rows.astype(jnp.bfloat16).reshape(owners, CAP, model_width)
    returned = lax.all_to_all(block_rows, "own", split_axis=0, concat_axis=0, tiled=True)
    per_slot = (
        returned.astype(jnp.float32)
        .reshape(experts_here, SPLIT, CAP, model_width)
        .sum(axis=1)
        .reshape(experts_here * CAP, model_width)
    )
    grad_tokens = jnp.dot(
        select, per_slot, precision=lax.Precision.HIGHEST, preferred_element_type=jnp.float32
    ).astype(jnp.bfloat16)
    stacked = jnp.stack([grad_gate, grad_up, grad_down]).astype(jnp.bfloat16).astype(jnp.float32)
    totals_all = lax.psum(stacked.astype(jnp.bfloat16), "rep").astype(jnp.float32)
    rows_each = stacked.shape[1] // lax.axis_size("rep")
    shares = lax.dynamic_slice_in_dim(totals_all, lax.axis_index("rep") * rows_each, rows_each, 1)
    return (grad_tokens, shares[0], shares[1], shares[2])


def solution(mesh):
    return jax.shard_map(
        per_device,
        mesh=mesh,
        in_specs=(
            P(("own", "rep"), None),
            P(("own", "rep"), None),
            P(("own", "rep"), None),
            P(("own", "rep"), None),
            P(),
            P(("own", "rep"), None),
            P(("own", "rep"), None),
            P(("own", "rep"), None),
        ),
        out_specs=(
            P(("own", "rep"), None),
            P(("own", "rep"), None),
            P(("own", "rep"), None),
            P(("own", "rep"), None),
        ),
        check_vma=False,
    )
```

profile of v0, /device:TPU:0, one launch (start us, length us, event | category | flops | bytes accessed | tf_op | source)
XLA Modules:
  0.0 113.1 jit_solution(7783864190615851945)
XLA Ops:
  7.2 0.0 copy-start
  7.2 0.0 copy-start.4
  7.2 0.0 all-gather.8.cloned.1.call-start
  7.2 0.7 all-gather.8.cloned.1.call-update
  7.9 0.0 all-gather.6.cloned.1.call-start
  8.0 0.7 all-gather.6.cloned.1.call-update
  8.7 0.0 copy-done.4
  8.7 0.1 copy.21
  8.8 0.1 eq.78
  8.9 0.1 eq.74
  9.1 1.6 %mul.53 = s32[128,6,24]{1,0,2:T(8,128)S(1)} reshape(s32[768,4,6]{0,2,1:T(8,128)S(1)} %mul.52) | data formatting | bytes 147456 | tf_op jit(solution)/shard_map/mul | solution.py:47
  10.7 1.1 %reduce-window.6 = s32[4,6,128]{2,1,0:T(8,128)S(1)} reduce-window(s32[4,6,128]{2,1,0:T(8,128)S(1)} %fusion.7, s32[]{:T(128)} %constant.6.clone.1), window={size=1x1x128 pad=0_0x0_0x127_0}, to_apply=%region_0.0 | reduce-window | flops 390144 | bytes 24580 | tf_op jit(solution)/shard_map/reduce-window
  11.9 0.2 slice_reduce_fusion
  12.1 0.2 reduce-window.9
  12.2 0.1 add_bitcast_fusion
  12.4 2.7 %eq.83 = s32[128,6,24]{1,0,2:T(8,128)} reshape(s32[768,4,6]{0,2,1:T(8,128)S(1)} %eq.82) | data formatting | bytes 147456 | tf_op jit(solution)/shard_map/eq | solution.py:48
  15.1 0.1 eq.85
  15.2 2.0 %convert_reduce_fusion = f32[128,24]{0,1:T(8,128)S(1)} fusion(s32[128,6,24]{1,0,2:T(8,128)S(1)} %mul.53, s32[128,6,24]{1,0,2:T(8,128)} %eq.83, s32[24]{0:T(128)S(1)} %eq.85), kind=kLoop, calls=%fused_computation.14 | loop fusion | flops 70656 | bytes 159840 | tf_op jit(solution)/shard_map/reduce_sum | solution.py:51
  17.2 0.0 copy-done
  17.2 0.2 convolution_convert_fusion.4
  17.4 0.0 copy-start.5
  17.4 0.0 copy-start.6
  17.4 0.0 copy-start.3
  17.5 0.9 broadcast_in_dim.11
  18.3 8.3 %all-to-all-start.1 = ((bf16[16,6,2560]{2,1,0:T(8,128)(2,1)}), bf16[16,6,2560]{2,1,0:T(8,128)(2,1)S(1)}, u32[]{:S(2)}, u32[]{:S(2)}) async-start(bf16[16,6,2560]{2,1,0:T(8,128)(2,1)} %bitcast.3), calls=%async_computation.1 | async-start | bytes 1310720 | tf_op jit(solution)/shard_map/all_to_all | solution.py:68
  26.7 0.0 copy-done.5
  26.7 0.0 copy-done.6
  26.7 0.3 select_reduce_fusion
  27.0 0.1 copy.23
  27.1 0.1 reshape.136
  27.3 0.2 convolution_bitcast_fusion
  27.4 0.2 fusion.4
  27.7 0.1 broadcast_in_dim.8
  27.7 16.3 %all-to-all-done.1 = bf16[16,6,2560]{2,1,0:T(8,128)(2,1)S(1)} async-done(((bf16[16,6,2560]{2,1,0:T(8,128)(2,1)}), bf16[16,6,2560]{2,1,0:T(8,128)(2,1)S(1)}, u32[]{:S(2)}, u32[]{:S(2)}) %all-to-all-start.1) | async-done | bytes 491552 | tf_op jit(solution)/shard_map/all_to_all | solution.py:68
  44.1 0.9 broadcast_in_dim.9
  45.0 4.4 %all-to-all-start = ((bf16[16,6,2560]{2,1,0:T(8,128)(2,1)}), bf16[16,6,2560]{2,1,0:T(8,128)(2,1)S(1)}, u32[]{:S(2)}, u32[]{:S(2)}) async-start(bf16[16,6,2560]{2,1,0:T(8,128)(2,1)} %bitcast.2), calls=%async_computation | async-start | bytes 1310720 | tf_op jit(solution)/shard_map/all_to_all | solution.py:69
  49.4 0.0 all-gather.4.cloned.1.call-start
  49.4 0.7 all-gather.4.cloned.1.call-update
  50.1 0.0 all-reduce.2.cloned.1.call-start
  50.2 0.2 reshape.129
  50.3 15.6 %all-to-all-done = bf16[16,6,2560]{2,1,0:T(8,128)(2,1)S(1)} async-done(((bf16[16,6,2560]{2,1,0:T(8,128)(2,1)}), bf16[16,6,2560]{2,1,0:T(8,128)(2,1)S(1)}, u32[]{:S(2)}, u32[]{:S(2)}) %all-to-all-start) | async-done | bytes 491552 | tf_op jit(solution)/shard_map/all_to_all | solution.py:69
  65.9 0.2 reshape.127
  66.1 0.0 all-gather.8.cloned.1.call-done
  66.1 1.8 %fusion.14 = f32[96,256]{1,0:T(8,128)S(1)} fusion(bf16[96,2560]{1,0:T(8,128)(2,1)S(1)} %reshape.129, bf16[256,2560]{1,0:T(8,128)(2,1)} %all-gather.8.cloned.1.call-done), kind=kOutput, calls=%fused_computation.41 | convolution fusion | flops 125829120 | bytes 1900544 | tf_op jit(solution)/shard_map/dot_general | solution.py:16
  67.9 0.0 all-gather.6.cloned.1.call-done
  68.0 1.8 %fusion.13 = f32[96,256]{1,0:T(8,128)S(1)} fusion(bf16[96,2560]{1,0:T(8,128)(2,1)S(1)} %reshape.129, bf16[256,2560]{1,0:T(8,128)(2,1)} %all-gather.6.cloned.1.call-done), kind=kOutput, calls=%fused_computation.40 | convolution fusion | flops 125829120 | bytes 1900544 | tf_op jit(solution)/shard_map/dot_general | solution.py:17
  69.8 0.5 fusion.2
  70.4 0.0 all-gather.4.cloned.1.call-done
  70.4 1.8 %multiply_convert_fusion.1 = (bf16[96,256]{1,0:T(8,128)(2,1)S(1)}, bf16[96,256]{1,0:T(8,128)(2,1)S(1)}) fusion(f32[96,256]{1,0:T(8,128)S(1)} %fusion.14, f32[96,256]{1,0:T(8,128)S(1)} %fusion.13, bf16[96,2560]{1,0:T(8,128)(2,1)S(1)} %reshape.127, bf16[256,2560]{1,0:T(8,128)(2,1)} %all-gather.4.cloned.1.call-done), kind=kOutput, calls=%fused_computation.23 | convolution fusion | flops 126148608 | bytes 2097152 | tf_op jit(solution)/shard_map/dot_general | solution.py:20
  72.2 0.5 fusion.1
  72.8 0.5 fusion
  73.3 2.1 %pad_maximum_fusion = bf16[3,256,2560]{2,1,0:T(8,128)(2,1)} fusion(bf16[1,256,2560]{2,1,0:T(8,128)(2,1)S(1)} %fusion.2, bf16[1,256,2560]{2,1,0:T(8,128)(2,1)S(1)} %fusion.1, bf16[1,256,2560]{2,1,0:T(8,128)(2,1)S(1)} %fusion), kind=kLoop, calls=%fused_computation | loop fusion | flops 3932160 | bytes 7864320 | tf_op jit(solution)/shard_map/stack | solution.py:92
  75.4 0.0 all-reduce.2.cloned.1.call-update
  75.4 1.3 %copy-done.1 = bf16[256,2560]{1,0:T(8,128)(2,1)S(1)} copy-done((bf16[256,2560]{1,0:T(8,128)(2,1)S(1)}, bf16[256,2560]{1,0:T(8,128)(2,1)}, u32[]{:S(2)}) %copy-start.1) | copy-done | bytes 1310744
  76.7 0.3 fusion.15
  77.1 1.0 copy-done.2
  78.0 0.3 fusion.3
  78.4 1.0 reshape.130
  79.4 4.4 %all-to-all-start.2 = ((bf16[16,6,2560]{2,1,0:T(8,128)(2,1)}), bf16[16,6,2560]{2,1,0:T(8,128)(2,1)S(1)}, u32[]{:S(2)}, u32[]{:S(2)}) async-start(bf16[16,6,2560]{2,1,0:T(8,128)(2,1)} %reshape.130), calls=%async_computation.2 | async-start | bytes 1310720 | tf_op jit(solution)/shard_map/all_to_all | solution.py:82
  83.8 16.5 %all-to-all-done.2 = bf16[16,6,2560]{2,1,0:T(8,128)(2,1)S(1)} async-done(((bf16[16,6,2560]{2,1,0:T(8,128)(2,1)}), bf16[16,6,2560]{2,1,0:T(8,128)(2,1)S(1)}, u32[]{:S(2)}, u32[]{:S(2)}) %all-to-all-start.2) | async-done | bytes 491552 | tf_op jit(solution)/shard_map/all_to_all | solution.py:82
  100.3 0.1 convert_reduce_fusion.1
  100.5 2.1 %convolution_convert_fusion.3 = bf16[128,2560]{1,0:T(8,128)(2,1)} fusion(f32[128,24]{0,1:T(8,128)S(1)} %convert_reduce_fusion, f32[24,2560]{1,0:T(8,128)S(1)} %reshape.133), kind=kOutput, calls=%fused_computation.8 | convolution fusion | flops 94699520 | bytes 913408 | tf_op jit(solution)/shard_map/dot_general | solution.py:89
  102.6 2.0 %dynamic-slice_convert_fusion = f32[3,128,2560]{2,1,0:T(8,128)S(1)} fusion(bf16[3,256,2560]{2,1,0:T(8,128)(2,1)} %all-reduce.2.cloned.1.call-done, s32[]{:T(128)S(6)} %select_n.3), kind=kLoop, calls=%fused_computation.13 | loop fusion | flops 983040 | bytes 5898244 | tf_op jit(solution)/shard_map/convert_element_type | solution.py:93
  104.6 2.0 %slice_bitcast_fusion = (f32[128,2560]{1,0:T(8,128)}, f32[128,2560]{1,0:T(8,128)}, f32[128,2560]{1,0:T(8,128)}) fusion(f32[3,128,2560]{2,1,0:T(8,128)S(1)} %dynamic-slice_convert_fusion), kind=kLoop, calls=%fused_computation.15 | loop fusion | bytes 7864320 | tf_op jit(solution)/shard_map/squeeze | solution.py:96
  (14 shorter events, 0.2 us)
Async XLA Ops:
  7.2 10.0 %copy-start = (bf16[128,2560]{1,0:T(8,128)(2,1)S(1)}, bf16[128,2560]{1,0:T(8,128)(2,1)}, u32[]{:S(2)}) copy-start(bf16[128,2560]{1,0:T(8,128)(2,1)} %param.8) | copy-start | bytes 1966084
  7.2 1.5 %copy-start.4 = (s32[128,6]{0,1:T(8,128)S(1)}, s32[128,6]{0,1:T(8,128)}, u32[]{:S(2)}) copy-start(s32[128,6]{0,1:T(8,128)} %param.10) | copy-start | bytes 9220
  7.2 58.9 %all-gather.8.cloned.1.call-start = ((), (), s32[]{:S(2)}) async-start(), calls=%async_computation.5 | async-start | bytes 1966080 | tf_op jit(solution)/shard_map/all_gather | solution.py:74
  7.9 60.0 %all-gather.6.cloned.1.call-start = ((), (), s32[]{:S(2)}) async-start(), calls=%async_computation.4 | async-start | bytes 1966080 | tf_op jit(solution)/shard_map/all_gather | solution.py:75
  17.4 9.3 %copy-start.5 = (s32[128,6]{0,1:T(8,128)S(1)}, s32[128,6]{0,1:T(8,128)}, u32[]{:S(2)}) copy-start(s32[128,6]{0,1:T(8,128)} %param.11) | copy-start | bytes 9220
  17.4 9.3 %copy-start.6 = (f32[256]{0:T(256)S(1)}, f32[256]{0:T(256)}, u32[]{:S(2)}) copy-start(f32[256]{0:T(256)} %param.12) | copy-start | bytes 3076
  17.4 10.0 %copy-start.3 = (bf16[128,2560]{1,0:T(8,128)(2,1)S(1)}, bf16[128,2560]{1,0:T(8,128)(2,1)}, u32[]{:S(2)}) copy-start(bf16[128,2560]{1,0:T(8,128)(2,1)} %param.9) | copy-start | bytes 1966084
  18.3 25.7 %all-to-all-start.1 = ((bf16[16,6,2560]{2,1,0:T(8,128)(2,1)}), bf16[16,6,2560]{2,1,0:T(8,128)(2,1)S(1)}, u32[]{:S(2)}, u32[]{:S(2)}) async-start(bf16[16,6,2560]{2,1,0:T(8,128)(2,1)} %bitcast.3), calls=%async_computation.1 | async-start | bytes 1310720 | tf_op jit(solution)/shard_map/all_to_all | solution.py:68
  45.0 21.0 %all-to-all-start = ((bf16[16,6,2560]{2,1,0:T(8,128)(2,1)}), bf16[16,6,2560]{2,1,0:T(8,128)(2,1)S(1)}, u32[]{:S(2)}, u32[]{:S(2)}) async-start(bf16[16,6,2560]{2,1,0:T(8,128)(2,1)} %bitcast.2), calls=%async_computation | async-start | bytes 1310720 | tf_op jit(solution)/shard_map/all_to_all | solution.py:69
  49.4 21.0 %all-gather.4.cloned.1.call-start = ((), (), s32[]{:S(2)}) async-start(), calls=%async_computation.3 | async-start | bytes 1966080 | tf_op jit(solution)/shard_map/all_gather | solution.py:76
  50.1 52.4 %all-reduce.2.cloned.1.call-start = ((), (), s32[]{:S(2)}) async-start(), calls=%async_computation.6 | async-start | bytes 7864320 | tf_op jit(solution)/shard_map/psum | solution.py:93
  75.4 1.3 %copy-start.1 = (bf16[256,2560]{1,0:T(8,128)(2,1)S(1)}, bf16[256,2560]{1,0:T(8,128)(2,1)}, u32[]{:S(2)}) copy-start(bf16[256,2560]{1,0:T(8,128)(2,1)} %all-gather.8.cloned.1.call-done) | copy-start | bytes 3932164
  76.7 1.3 %copy-start.2 = (bf16[256,2560]{1,0:T(8,128)(2,1)S(1)}, bf16[256,2560]{1,0:T(8,128)(2,1)}, u32[]{:S(2)}) copy-start(bf16[256,2560]{1,0:T(8,128)(2,1)} %all-gather.6.cloned.1.call-done) | copy-start | bytes 3932164
  79.4 20.9 %all-to-all-start.2 = ((bf16[16,6,2560]{2,1,0:T(8,128)(2,1)}), bf16[16,6,2560]{2,1,0:T(8,128)(2,1)S(1)}, u32[]{:S(2)}, u32[]{:S(2)}) async-start(bf16[16,6,2560]{2,1,0:T(8,128)(2,1)} %reshape.130), calls=%async_computation.2 | async-start | bytes 1310720 | tf_op jit(solution)/shard_map/all_to_all | solution.py:82
Sparse Core Ops, SparseCore 0:
  9.6 12.1 all-gather.7
  23.3 10.5 all-gather.5
  51.8 10.7 all-gather.3
  75.5 23.4 all-reduce.1
where the time goes:
time: 114 us; the launch traced here: 113 us
  waiting for transfers between devices  50.6 us (44%)
  starting transfers between devices  17.3 us (15%)
  between operations  14.1 us (12%)
  local copies, waits for them, and re-layouts  12.8 us (11%)
  matrix products  10.4 us (9%)
  other arithmetic  7.96 us (7%)
    all_to_all x1, waiting for transfers between devices, per_device(): lax.all_to_all(block_rows, 'own', split_axis=0, concat_axis=0, tiled=True)  16.5 us
    all_to_all x1, waiting for transfers between devices, per_device(): lax.all_to_all(fan_out(sent_x), 'own', split_axis=0, concat_axis=0, tiled...  16.3 us
    all_to_all x1, waiting for transfers between devices, per_device(): lax.all_to_all(fan_out(sent_cot), 'own', split_axis=0, concat_axis=0, til...  15.6 us
    all_to_all x1, starting transfers between devices, per_device(): lax.all_to_all(fan_out(sent_x), 'own', split_axis=0, concat_axis=0, tiled...  8.31 us
    all_to_all x1, starting transfers between devices, per_device(): lax.all_to_all(fan_out(sent_cot), 'own', split_axis=0, concat_axis=0, til...  4.42 us
    all_to_all x1, starting transfers between devices, per_device(): lax.all_to_all(block_rows, 'own', split_axis=0, concat_axis=0, tiled=True)  4.37 us
    eq x4, local copies, waits for them, and re-layouts, per_device(): earlier[:, :, None] == jnp.arange(CAP, dtype=jnp.int32)[None, None, :]  2.84 us
    unnamed x15, local copies, waits for them, and re-layouts  2.4 us
  transfers between devices with their start and end apart: 7, of which 3 were waited for; matrix products, arithmetic and copies ran while one was open for 18% of the time, Pallas kernels for 0%

commit v1 on v0

--- a/solution.py
+++ b/solution.py
@@ -2,6 +2,9 @@
 import jax.numpy as jnp
 from jax import lax
 from jax.sharding import PartitionSpec as P
+
+from jax.experimental import pallas as pl
+from jax.experimental.pallas import tpu as pltpu
 
 SPLIT = 4
 CAP = 6
@@ -42,7 +45,12 @@
     is_named = (
         route.reshape(-1)[:, None] == jnp.arange(experts_here, dtype=jnp.int32)[None, :]
     ).astype(jnp.int32)
-    earlier = jnp.cumsum(is_named, axis=0) - is_named
+    pair_ids = jnp.arange(is_named.shape[0], dtype=jnp.int32)
+    earlier = jnp.dot(
+        (pair_ids[:, None] > pair_ids[None, :]).astype(jnp.bfloat16),
+        is_named.astype(jnp.bfloat16),
+        preferred_element_type=jnp.float32,
+    ).astype(jnp.int32)
     slot_hits = (
         is_named[:, :, None]
         * (earlier[:, :, None] == jnp.arange(CAP, dtype=jnp.int32)[None, None, :]).astype(jnp.int32)
@@ -96,9 +104,318 @@
     return (grad_tokens, shares[0], shares[1], shares[2])
 
 
+MESH = pl.DeviceIdType.MESH
+F32 = jnp.float32
+BF16 = jnp.bfloat16
+SLOT_ROWS = 8
+BLOCK = 2 * SLOT_ROWS
+PLANE = 4
+DEPTH = 4
+
+
+def flip(value, bit):
+    return value + bit - 2 * bit * lax.rem(lax.div(value, bit), 2)
+
+
+def flipped(value, pattern):
+    for bit in (1, 2):
+        if pattern & bit:
+            value = flip(value, bit)
+    return value
+
+
+def kernel(
+    route_ref, gidx_ref, table_ref, tok_hbm, cot_hbm, wg_hbm, wu_hbm, wd_hbm,
+    ps_out, sel_out, wgrad_out,
+    tok, cot, w, sbuf, rows, delta, acc, pa_s, pa_r, bx_s, bx_r, by_s, by_r,
+    cx_s, cx_r, cy_s, cy_r, zs_s, zs_r, wgrad,
+    in_sem, out_sem, send_sem, recv_sem,
+):
+    own = lax.axis_index("own")
+    rep = lax.axis_index("rep")
+    z = lax.div(own, PLANE)
+    s = lax.rem(own, PLANE)
+    width = tok.shape[1]
+    half = width // 2
+    units = wg_hbm.shape[0]
+
+    loads = [
+        pltpu.make_async_copy(tok_hbm, tok, in_sem.at[0]),
+        pltpu.make_async_copy(cot_hbm, cot, in_sem.at[1]),
+        pltpu.make_async_copy(wg_hbm, w.at[pl.ds(0, units)], in_sem.at[2]),
+        pltpu.make_async_copy(wu_hbm, w.at[pl.ds(units, units)], in_sem.at[3]),
+        pltpu.make_async_copy(wd_hbm, w.at[pl.ds(2 * units, units)], in_sem.at[4]),
+    ]
+    for load in loads:
+        load.start()
+
+    dev_z = [None] + [(flipped(z, k) * PLANE + s, rep) for k in range(1, DEPTH)]
+    dev_x = (z * PLANE + flip(s, 1), rep)
+    dev_y = (z * PLANE + flip(s, 2), rep)
+    dev_p = (own, 1 - rep)
+    barrier = pltpu.get_barrier_semaphore()
+    for device in dev_z[1:] + [dev_x, dev_y, dev_p]:
+        pl.semaphore_signal(barrier, inc=1, device_id=device, device_id_type=MESH)
+
+    number = iter(range(64))
+
+    def remote(src, dst, device):
+        i = next(number)
+        return pltpu.make_async_remote_copy(
+            src_ref=src, dst_ref=dst, send_sem=send_sem.at[i], recv_sem=recv_sem.at[i],
+            device_id=device, device_id_type=MESH,
+        )
+
+    lo, hi = pl.ds(0, half), pl.ds(half, half)
+    ks_all = range(DEPTH)
+    c_z = [None] + [remote(sbuf.at[k - 1], rows.at[0, 0, k], dev_z[k]) for k in range(1, DEPTH)]
+    c_x = [remote(rows.at[0, 0, k], rows.at[1, 0, k], dev_x) for k in ks_all]
+    c_y = [remote(rows.at[0, 0, k], rows.at[2, 0, k], dev_y) for k in ks_all]
+    c_rx = [remote(rows.at[2, 0, k, :, hi], rows.at[3, 0, k, :, hi], dev_x) for k in ks_all]
+    c_ry = [remote(rows.at[1, 0, k, :, lo], rows.at[3, 0, k, :, lo], dev_y) for k in ks_all]
+    c_p = [[remote(rows.at[q, 0, k], rows.at[q, 1, k], dev_p) for k in ks_all] for q in range(PLANE)]
+    c_pa = [remote(pa_s.at[q], pa_r.at[q], dev_p) for q in range(PLANE)]
+    c_bx = [remote(bx_s.at[q], bx_r.at[q], dev_x) for q in range(2)]
+    c_by = [remote(by_s.at[q], by_r.at[q], dev_y) for q in range(2)]
+    c_cx = remote(cx_s, cx_r, dev_x)
+    c_cy = remote(cy_s, cy_r, dev_y)
+    c_zs = [None] + [remote(zs_s.at[k - 1], zs_r.at[k - 1], dev_z[k]) for k in range(1, DEPTH)]
+
+    count, choices = route_ref.shape
+    lane = lax.broadcasted_iota(jnp.int32, (1, 128), 1)
+    which = lax.div(lane, SLOT_ROWS)
+    slot = lax.rem(lane, SLOT_ROWS)
+    low, high = lax.rem(which, 2), lax.div(which, 2)
+    z_low, z_high = lax.rem(z, 2), lax.div(z, 2)
+    expert = (low + z_low - 2 * low * z_low) + 2 * (high + z_high - 2 * high * z_high)
+    expert = jnp.where(which < DEPTH, expert, -1)
+    named = jnp.zeros((count, 128), F32)
+    entry = jnp.zeros((count, 128), F32)
+    for choice in range(choices):
+        hit = route_ref[:, choice : choice + 1] == expert
+        named = named + jnp.where(hit, 1.0, 0.0)
+        entry = entry + jnp.where(hit, gidx_ref[:, choice : choice + 1].astype(F32), 0.0)
+    below = (
+        lax.broadcasted_iota(jnp.int32, (count, count), 0)
+        > lax.broadcasted_iota(jnp.int32, (count, count), 1)
+    )
+    earlier = jnp.dot(
+        jnp.where(below, 1.0, 0.0).astype(BF16), named.astype(BF16), preferred_element_type=F32
+    )
+    select = jnp.where(earlier == slot.astype(F32), named, 0.0)
+    sel_out[...] = select.astype(BF16)
+    slots = DEPTH * SLOT_ROWS
+    picker = select.T[:slots].astype(BF16)
+    slot_entry = jnp.sum((select * entry).T[:slots], axis=1, keepdims=True)
+    table_at = lax.broadcasted_iota(jnp.int32, (slots, table_ref.shape[1]), 1).astype(F32)
+    slot_gate = jnp.sum(jnp.where(table_at == slot_entry, table_ref[...], 0.0), axis=1, keepdims=True)
+
+    loads[0].wait()
+    picked_x = jnp.dot(picker, tok[...], preferred_element_type=F32)
+    loads[1].wait()
+    picked_cot = slot_gate * jnp.dot(picker, cot[...], preferred_element_type=F32)
+
+    def block(k):
+        at = slice(k * SLOT_ROWS, (k + 1) * SLOT_ROWS)
+        return jnp.concatenate([picked_x[at], picked_cot[at]], axis=0).astype(BF16)
+
+    for k in range(1, DEPTH):
+        sbuf[k - 1] = block(k)
+    rows[0, 0, 0] = block(0)
+    pl.semaphore_wait(barrier, 6)
+
+    def spread(k):
+        c_x[k].start()
+        c_y[k].start()
+        c_p[0][k].start()
+
+    def relay(k):
+        c_x[k].wait_recv()
+        c_ry[k].start()
+        c_p[1][k].start()
+        c_y[k].wait_recv()
+        c_rx[k].start()
+        c_p[2][k].start()
+
+    for k in (3, 1, 2):
+        c_z[k].start()
+    spread(0)
+    for load in loads[2:]:
+        load.wait()
+    c_z[1].wait_recv()
+    spread(1)
+    relay(0)
+    c_z[2].wait_recv()
+    spread(2)
+    relay(1)
+    c_z[3].wait_recv()
+    spread(3)
+    relay(2)
+    relay(3)
+
+    def piece(q):
+        for k in ks_all:
+            c_p[q][k].wait_recv()
+        pre = lax.dot_general(
+            rows[q].reshape(2 * DEPTH * BLOCK, width), w[...],
+            (((1,), (1,)), ((), ())), preferred_element_type=F32,
+        ).reshape(2 * DEPTH, BLOCK, 3 * units)
+        pre_x = pre[:, :SLOT_ROWS].reshape(2 * slots, 3 * units)
+        pre_c = pre[:, SLOT_ROWS:].reshape(2 * slots, 3 * units)
+        gate, up, hidden_delta = pre_x[:, :units], pre_x[:, units : 2 * units], pre_c[:, 2 * units :]
+        sig = jax.nn.sigmoid(gate)
+        active = gate * sig
+        hidden = active * up
+        gate_delta = hidden_delta * up * (sig * (1.0 + gate * (1.0 - sig)))
+        up_delta = hidden_delta * active
+        both = jnp.concatenate([gate_delta, up_delta], axis=1)
+        back = jnp.dot(both.astype(BF16), w[: 2 * units], preferred_element_type=F32)
+        pa_s[q] = back[slots:].astype(BF16)
+        c_pa[q].start()
+        acc[q] = back[:slots]
+        none = jnp.zeros((2 * DEPTH, SLOT_ROWS, units), F32)
+
+        def placed(values, first):
+            values = values.reshape(2 * DEPTH, SLOT_ROWS, units)
+            pair = [values, none] if first else [none, values]
+            return jnp.concatenate(pair, axis=1).reshape(2 * DEPTH * BLOCK, units)
+
+        full = jnp.concatenate(
+            [placed(gate_delta, True), placed(up_delta, True), placed(hidden, False)], axis=1
+        )
+        delta[q * 2 * DEPTH * BLOCK : (q + 1) * 2 * DEPTH * BLOCK] = full.astype(BF16)
+
+    piece(0)
+    for k in ks_all:
+        c_ry[k].wait_recv()
+        c_rx[k].wait_recv()
+        c_p[3][k].start()
+    piece(1)
+    piece(2)
+    piece(3)
+
+    chunks = wgrad_out.shape[1] // 512
+    stores = [
+        pltpu.make_async_copy(
+            wgrad.at[:, pl.ds(512 * n, 512)], wgrad_out.at[:, pl.ds(512 * n, 512)], out_sem.at[n]
+        )
+        for n in range(chunks)
+    ]
+
+    def weights(n):
+        at = slice(512 * n, 512 * (n + 1))
+        right = rows[:, :, :, :, at].reshape(PLANE * 2 * DEPTH * BLOCK, 512)
+        wgrad[:, at] = lax.dot_general(
+            delta[...], right, (((0,), (0,)), ((), ())), preferred_element_type=F32
+        ).astype(BF16)
+        stores[n].start()
+
+    def merged(q):
+        c_pa[q].wait_recv()
+        return acc[q] + pa_r[q].astype(F32)
+
+    one = merged(1)
+    bx_s[0] = one[:, :half].astype(BF16)
+    c_bx[0].start()
+    acc[1] = one
+    two = merged(2)
+    by_s[0] = two[:, half:].astype(BF16)
+    c_by[0].start()
+    acc[2] = two
+    three = merged(3)
+    bx_s[1] = three[:, :half].astype(BF16)
+    c_bx[1].start()
+    by_s[1] = three[:, half:].astype(BF16)
+    c_by[1].start()
+    acc[0] = merged(0)
+    for n in range(0, chunks - 2):
+        weights(n)
+    c_bx[1].wait_recv()
+    cy_s[...] = (acc[2, :, :half] + bx_r[1].astype(F32)).astype(BF16)
+    c_cy.start()
+    c_by[1].wait_recv()
+    cx_s[...] = (acc[1, :, half:] + by_r[1].astype(F32)).astype(BF16)
+    c_cx.start()
+    weights(chunks - 2)
+    c_bx[0].wait_recv()
+    c_by[0].wait_recv()
+    c_cy.wait_recv()
+    c_cx.wait_recv()
+    left = acc[0, :, :half] + bx_r[0].astype(F32) + cy_r[...].astype(F32)
+    right = acc[0, :, half:] + by_r[0].astype(F32) + cx_r[...].astype(F32)
+    for k in (3, 1, 2):
+        at = slice(k * SLOT_ROWS, (k + 1) * SLOT_ROWS)
+        zs_s[k - 1] = jnp.concatenate([left[at], right[at]], axis=0).astype(BF16)
+        c_zs[k].start()
+    weights(chunks - 1)
+    parts = [jnp.concatenate([left[:SLOT_ROWS], right[:SLOT_ROWS]], axis=1)]
+    for k in range(1, DEPTH):
+        c_zs[k].wait_recv()
+        got = zs_r[k - 1].astype(F32)
+        parts.append(jnp.concatenate([got[:SLOT_ROWS], got[SLOT_ROWS:]], axis=1))
+    ps_out[...] = jnp.concatenate(parts, axis=0).astype(BF16)
+
+    for copy in c_z[1:] + c_x + c_y + c_rx + c_ry + sum(c_p, []) + c_pa + c_bx + c_by:
+        copy.wait_send()
+    for copy in [c_cx, c_cy] + c_zs[1:]:
+        copy.wait_send()
+    for store in stores:
+        store.wait()
+
+
+def per_device_fast(tokens, cotangent, route, gate_index, gate_table, w_gate, w_up, w_down):
+    count, width = tokens.shape
+    units = w_gate.shape[0]
+    half = width // 2
+    slots = DEPTH * SLOT_ROWS
+    vmem = pl.BlockSpec(memory_space=pltpu.VMEM)
+    hbm = pl.BlockSpec(memory_space=pltpu.HBM)
+    slot_grads, select, weight_grads = pl.pallas_call(
+        kernel,
+        out_shape=(
+            jax.ShapeDtypeStruct((slots, width), BF16),
+            jax.ShapeDtypeStruct((count, 128), BF16),
+            jax.ShapeDtypeStruct((3 * units, width), BF16),
+        ),
+        in_specs=[vmem] * 3 + [hbm] * 5,
+        out_specs=(vmem, vmem, pl.BlockSpec(memory_space=pl.ANY)),
+        scratch_shapes=[
+            pltpu.VMEM((count, width), BF16),
+            pltpu.VMEM((count, width), BF16),
+            pltpu.VMEM((3 * units, width), BF16),
+            pltpu.VMEM((DEPTH - 1, BLOCK, width), BF16),
+            pltpu.VMEM((PLANE, 2, DEPTH, BLOCK, width), BF16),
+            pltpu.VMEM((PLANE * 2 * DEPTH * BLOCK, 3 * units), BF16),
+            pltpu.VMEM((PLANE, slots, width), F32),
+            pltpu.VMEM((PLANE, slots, width), BF16),
+            pltpu.VMEM((PLANE, slots, width), BF16),
+        ]
+        + [pltpu.VMEM((2, slots, half), BF16)] * 4
+        + [pltpu.VMEM((slots, half), BF16)] * 4
+        + [pltpu.VMEM((DEPTH - 1, BLOCK, half), BF16)] * 2
+        + [
+            pltpu.VMEM((3 * units, width), BF16),
+            pltpu.SemaphoreType.DMA((5,)),
+            pltpu.SemaphoreType.DMA((width // 512,)),
+            pltpu.SemaphoreType.DMA((52,)),
+            pltpu.SemaphoreType.DMA((52,)),
+        ],
+        compiler_params=pltpu.CompilerParams(
+            collective_id=0, has_side_effects=True, vmem_limit_bytes=40 * 1024 * 1024
+        ),
+    )(route, gate_index, gate_table.reshape(1, -1), tokens, cotangent, w_gate, w_up, w_down)
+    grad_tokens = jnp.dot(
+        select[:, :slots], slot_grads, preferred_element_type=jnp.float32
+    ).astype(jnp.bfloat16)
+    wide = weight_grads.astype(jnp.float32)
+    return (grad_tokens, wide[:units], wide[units : 2 * units], wide[2 * units :])
+
+
 def solution(mesh):
+    one_plane_each = mesh.shape["own"] == DEPTH * PLANE and mesh.shape["rep"] == 2
+    body = per_device_fast if one_plane_each else per_device
     return jax.shard_map(
-        per_device,
+        body,
         mesh=mesh,
         in_specs=(
             P(("own", "rep"), None),

time: 114 us -> 55.1 us (0.48)
  waiting for transfers between devices: 50.6 us -> 0 us
  Pallas kernels: 0 us -> 43.2 us
  starting transfers between devices: 17.3 us -> 0 us
  between operations: 14.1 us -> 0.65 us
  matrix products: 10.4 us -> 1.14 us
  other arithmetic: 7.96 us -> 0 us
  local copies, waits for them, and re-layouts: 12.8 us -> 9.75 us
    all_to_all x3 -> x0, waiting for transfers between devices: 48.4 us -> none  [the longest x1 16.5 us: per_device(): lax.all_to_all(block_rows, 'own', split_axis=0, concat_axis=0, tiled=True)]
    pallas_call x0 -> x1, Pallas kernels: none -> 43.2 us  [per_device_fast(): pl.pallas_call(kernel, out_shape=(jax.ShapeDtypeStruct((slots, width), BF...]
    all_to_all x3 -> x0, starting transfers between devices: 17.1 us -> none  [the longest x1 8.31 us: per_device(): lax.all_to_all(fan_out(sent_x), 'own', split_axis=0, concat_axis=0, tiled...]
    dot_general x12 -> x1, matrix products: 10.4 us -> 1.14 us  [per_device_fast(): jnp.dot(select[:, :slots], slot_grads, preferred_element_type=jnp.float32)]
    unnamed x15 -> x14, local copies, waits for them, and re-layouts: 2.4 us -> 7.69 us
    another operation x3 -> x0, other arithmetic: 3.43 us -> none  [the longest x1 2.1 us: per_device(): jnp.stack([grad_gate, grad_up, grad_down]).astype(jnp.bfloat16)]
    eq x6 -> x0, local copies, waits for them, and re-layouts: 3.11 us -> none  [the longest x4 2.84 us: per_device(): earlier[:, :, None] == jnp.arange(CAP, dtype=jnp.int32)[None, None, :]]
    reduce_sum x3 -> x0, other arithmetic: 2.4 us -> none  [the longest x1 1.95 us: per_device(): slot_hits.reshape(tok_count, choices_each, experts_here * CAP).sum(axis=1)]
  transfers between devices with their start and end apart: 7 -> 0, of which waited for: 3 -> 0; matrix products, arithmetic and copies ran while one was open for 18% -> 0% of each run, Pallas kernels for 0% -> 0%
where the time goes in v1:
time: 55.1 us; the launch traced here: 54.7 us
  Pallas kernels  43.2 us (78%)
  local copies, waits for them, and re-layouts  9.75 us (18%)
  matrix products  1.14 us (2%)
  between operations  0.65 us (1%)
    pallas_call x1, Pallas kernels, per_device_fast(): pl.pallas_call(kernel, out_shape=(jax.ShapeDtypeStruct((slots, width), BF...  43.2 us
    unnamed x14, local copies, waits for them, and re-layouts  7.69 us
    slice x1, local copies, waits for them, and re-layouts, per_device_fast(): return (grad_tokens, wide[:units], wide[units:2 * units], wide[2 * units:])  2.05 us
    dot_general x1, matrix products, per_device_fast(): jnp.dot(select[:, :slots], slot_grads, preferred_element_type=jnp.float32)  1.14 us

profile of v1, /device:TPU:0, one launch (start us, length us, event | category | flops | bytes accessed | tf_op | source)
XLA Modules:
  0.0 54.7 jit_solution(496967091567222816)
XLA Ops:
  0.6 0.8 %copy.12.route_ref = s32[128,6]{1,0:T(8,128)S(1)} copy(s32[128,6]{0,1:T(8,128)} %param.10) | data formatting | bytes 6144 | tf_op args[2]
  1.4 0.8 %copy.13.gidx_ref = s32[128,6]{1,0:T(8,128)S(1)} copy(s32[128,6]{0,1:T(8,128)} %param.11) | data formatting | bytes 6144 | tf_op args[3]
  2.2 0.0 copy-start
  2.2 1.1 %copy-done = bf16[128,2560]{1,0:T(8,128)(2,1)S(1)} copy-done((bf16[128,2560]{1,0:T(8,128)(2,1)S(1)}, bf16[128,2560]{1,0:T(8,128)(2,1)}, u32[]{:S(2)}) %copy-start) | copy-done | bytes 655384
  3.3 0.0 copy-start.1
  3.3 1.1 %copy-done.1 = bf16[128,2560]{1,0:T(8,128)(2,1)S(1)} copy-done((bf16[128,2560]{1,0:T(8,128)(2,1)S(1)}, bf16[128,2560]{1,0:T(8,128)(2,1)}, u32[]{:S(2)}) %copy-start.1) | copy-done | bytes 655384
  4.4 0.0 copy-start.2
  4.4 1.1 %copy-done.2 = bf16[128,2560]{1,0:T(8,128)(2,1)S(1)} copy-done((bf16[128,2560]{1,0:T(8,128)(2,1)S(1)}, bf16[128,2560]{1,0:T(8,128)(2,1)}, u32[]{:S(2)}) %copy-start.2) | copy-done | bytes 655384
  5.5 0.0 copy-start.3
  5.5 1.1 %copy-done.3 = bf16[128,2560]{1,0:T(8,128)(2,1)S(1)} copy-done((bf16[128,2560]{1,0:T(8,128)(2,1)S(1)}, bf16[128,2560]{1,0:T(8,128)(2,1)}, u32[]{:S(2)}) %copy-start.3) | copy-done | bytes 655384
  6.6 0.0 copy-start.4
  6.6 1.1 %copy-done.4 = bf16[128,2560]{1,0:T(8,128)(2,1)S(1)} copy-done((bf16[128,2560]{1,0:T(8,128)(2,1)S(1)}, bf16[128,2560]{1,0:T(8,128)(2,1)}, u32[]{:S(2)}) %copy-start.4) | copy-done | bytes 655384
  7.7 0.0 copy-start.5
  7.7 0.7 %copy-done.5 = f32[256]{0:T(256)S(1)} copy-done((f32[256]{0:T(256)S(1)}, f32[256]{0:T(256)}, u32[]{:S(2)}) %copy-start.5) | copy-done | bytes 1048
  8.3 43.2 %shard_map.111 = (bf16[32,2560]{1,0:T(8,128)(2,1)S(1)}, bf16[128,128]{1,0:T(8,128)(2,1)S(1)}, bf16[384,2560]{1,0:T(8,128)(2,1)S(1)}) custom-call(s32[128,6]{1,0:T(8,128)S(1)} %copy.12.route_ref, s32[128,6]{1,0:T(8,128)S(1)} %copy.13.gidx_ref, f32[1,256]{1,0:T(1,128)S(1)} %bitcast.2, bf16[128,2560]{1,0:T(8,128)(2,1)S(1)} %copy-done, ...), custom_call_target="tpu_custom_call" | custom-call | tf_op jit(solution)/shard_map/pallas_call | solution.py:373
  51.5 2.1 %fusion.1 = (f32[128,2560]{1,0:T(8,128)}, f32[128,2560]{1,0:T(8,128)}, f32[128,2560]{1,0:T(8,128)}) fusion(bf16[384,2560]{1,0:T(8,128)(2,1)S(1)} %get-tuple-element.9), kind=kLoop, calls=%fused_computation.2 | loop fusion | bytes 7864320 | tf_op jit(solution)/shard_map/slice | solution.py:411
  53.6 1.1 %convolution_convert_fusion = bf16[128,2560]{1,0:T(8,128)(2,1)} fusion(bf16[32,2560]{1,0:T(8,128)(2,1)S(1)} %get-tuple-element.8, bf16[128,128]{1,0:T(8,128)(2,1)S(1)} %get-tuple-element.7), kind=kOutput, calls=%fused_computation | convolution fusion | flops 21299200 | bytes 851968 | tf_op jit(solution)/shard_map/dot_general | solution.py:407
Async XLA Ops:
  2.2 1.1 %copy-start = (bf16[128,2560]{1,0:T(8,128)(2,1)S(1)}, bf16[128,2560]{1,0:T(8,128)(2,1)}, u32[]{:S(2)}) copy-start(bf16[128,2560]{1,0:T(8,128)(2,1)} %tok_hbm.1) | copy-start | bytes 1966084
  3.3 1.1 %copy-start.1 = (bf16[128,2560]{1,0:T(8,128)(2,1)S(1)}, bf16[128,2560]{1,0:T(8,128)(2,1)}, u32[]{:S(2)}) copy-start(bf16[128,2560]{1,0:T(8,128)(2,1)} %cot_hbm.1) | copy-start | bytes 1966084
  4.4 1.1 %copy-start.2 = (bf16[128,2560]{1,0:T(8,128)(2,1)S(1)}, bf16[128,2560]{1,0:T(8,128)(2,1)}, u32[]{:S(2)}) copy-start(bf16[128,2560]{1,0:T(8,128)(2,1)} %wg_hbm.1) | copy-start | bytes 1966084
  5.5 1.1 %copy-start.3 = (bf16[128,2560]{1,0:T(8,128)(2,1)S(1)}, bf16[128,2560]{1,0:T(8,128)(2,1)}, u32[]{:S(2)}) copy-start(bf16[128,2560]{1,0:T(8,128)(2,1)} %wu_hbm.1) | copy-start | bytes 1966084
  6.6 1.1 %copy-start.4 = (bf16[128,2560]{1,0:T(8,128)(2,1)S(1)}, bf16[128,2560]{1,0:T(8,128)(2,1)}, u32[]{:S(2)}) copy-start(bf16[128,2560]{1,0:T(8,128)(2,1)} %wd_hbm.1) | copy-start | bytes 1966084
  7.7 0.7 %copy-start.5 = (f32[256]{0:T(256)S(1)}, f32[256]{0:T(256)}, u32[]{:S(2)}) copy-start(f32[256]{0:T(256)} %param.12) | copy-start | bytes 3076

commit v2 on v1

--- a/solution.py
+++ b/solution.py
@@ -107,10 +107,12 @@
 MESH = pl.DeviceIdType.MESH
 F32 = jnp.float32
 BF16 = jnp.bfloat16
+SLOTS = CAP
 SLOT_ROWS = 8
 BLOCK = 2 * SLOT_ROWS
 PLANE = 4
 DEPTH = 4
+VMEM_BYTES = 62 * 1024 * 1024
 
 
 def flip(value, bit):
@@ -125,9 +127,9 @@
 
 
 def kernel(
-    route_ref, gidx_ref, table_ref, tok_hbm, cot_hbm, wg_hbm, wu_hbm, wd_hbm,
-    ps_out, sel_out, wgrad_out,
-    tok, cot, w, sbuf, rows, delta, acc, pa_s, pa_r, bx_s, bx_r, by_s, by_r,
+    route_hbm, gidx_hbm, table_hbm, tok_hbm, cot_hbm, wg_hbm, wu_hbm, wd_hbm,
+    tokens_out, wgrad_out,
+    route_ref, gidx_ref, table_ref, tok, cot, w, sbuf, rows, tails, delta, acc, pa_s, pa_r, bx_s, bx_r, by_s, by_r,
     cx_s, cx_r, cy_s, cy_r, zs_s, zs_r, wgrad,
     in_sem, out_sem, send_sem, recv_sem,
 ):
@@ -136,9 +138,16 @@
     z = lax.div(own, PLANE)
     s = lax.rem(own, PLANE)
     width = tok.shape[1]
-    half = width // 2
+    tail = width // 4
+    packed = 3 * tail
+    cut = bx_s.shape[2]
     units = wg_hbm.shape[0]
 
+    small = [
+        pltpu.make_async_copy(route_hbm, route_ref, in_sem.at[5]),
+        pltpu.make_async_copy(gidx_hbm, gidx_ref, in_sem.at[6]),
+        pltpu.make_async_copy(table_hbm, table_ref, in_sem.at[7]),
+    ]
     loads = [
         pltpu.make_async_copy(tok_hbm, tok, in_sem.at[0]),
         pltpu.make_async_copy(cot_hbm, cot, in_sem.at[1]),
@@ -146,7 +155,7 @@
         pltpu.make_async_copy(wu_hbm, w.at[pl.ds(units, units)], in_sem.at[3]),
         pltpu.make_async_copy(wd_hbm, w.at[pl.ds(2 * units, units)], in_sem.at[4]),
     ]
-    for load in loads:
+    for load in small + loads:
         load.start()
 
     dev_z = [None] + [(flipped(z, k) * PLANE + s, rep) for k in range(1, DEPTH)]
@@ -166,7 +175,7 @@
             device_id=device, device_id_type=MESH,
         )
 
-    lo, hi = pl.ds(0, half), pl.ds(half, half)
+    lo, hi = pl.ds(0, cut), pl.ds(cut, packed - cut)
     ks_all = range(DEPTH)
     c_z = [None] + [remote(sbuf.at[k - 1], rows.at[0, 0, k], dev_z[k]) for k in range(1, DEPTH)]
     c_x = [remote(rows.at[0, 0, k], rows.at[1, 0, k], dev_x) for k in ks_all]
@@ -181,47 +190,62 @@
     c_cy = remote(cy_s, cy_r, dev_y)
     c_zs = [None] + [remote(zs_s.at[k - 1], zs_r.at[k - 1], dev_z[k]) for k in range(1, DEPTH)]
 
-    count, choices = route_ref.shape
-    lane = lax.broadcasted_iota(jnp.int32, (1, 128), 1)
-    which = lax.div(lane, SLOT_ROWS)
-    slot = lax.rem(lane, SLOT_ROWS)
+    choices, count = route_ref.shape
+    slots = DEPTH * SLOT_ROWS
+    line = lax.broadcasted_iota(jnp.int32, (slots, 1), 0)
+    which = lax.div(line, SLOT_ROWS)
+    slot = lax.rem(line, SLOT_ROWS)
     low, high = lax.rem(which, 2), lax.div(which, 2)
     z_low, z_high = lax.rem(z, 2), lax.div(z, 2)
     expert = (low + z_low - 2 * low * z_low) + 2 * (high + z_high - 2 * high * z_high)
-    expert = jnp.where(which < DEPTH, expert, -1)
-    named = jnp.zeros((count, 128), F32)
-    entry = jnp.zeros((count, 128), F32)
+    for load in small:
+        load.wait()
+    named = jnp.zeros((slots, count), F32)
+    entry = jnp.zeros((slots, count), F32)
     for choice in range(choices):
-        hit = route_ref[:, choice : choice + 1] == expert
+        hit = route_ref[choice : choice + 1, :] == expert
         named = named + jnp.where(hit, 1.0, 0.0)
-        entry = entry + jnp.where(hit, gidx_ref[:, choice : choice + 1].astype(F32), 0.0)
-    below = (
+        entry = entry + jnp.where(hit, gidx_ref[choice : choice + 1, :].astype(F32), 0.0)
+    before = (
         lax.broadcasted_iota(jnp.int32, (count, count), 0)
-        > lax.broadcasted_iota(jnp.int32, (count, count), 1)
+        < lax.broadcasted_iota(jnp.int32, (count, count), 1)
     )
     earlier = jnp.dot(
-        jnp.where(below, 1.0, 0.0).astype(BF16), named.astype(BF16), preferred_element_type=F32
-    )
-    select = jnp.where(earlier == slot.astype(F32), named, 0.0)
-    sel_out[...] = select.astype(BF16)
-    slots = DEPTH * SLOT_ROWS
-    picker = select.T[:slots].astype(BF16)
-    slot_entry = jnp.sum((select * entry).T[:slots], axis=1, keepdims=True)
+        named.astype(BF16), jnp.where(before, 1.0, 0.0).astype(BF16), preferred_element_type=F32
+    )
+    thirds = range(3)
+    spare = slot >= SLOTS
+
+    def pick(number, rows_on):
+        return jnp.where((earlier == number.astype(F32)) & rows_on, named, 0.0)
+
+    select = pick(slot, slot < SLOTS)
+    spill = [pick(3 * (slot - SLOTS) + n, spare) for n in thirds]
+    pickers = [jnp.concatenate([select, spill[n]], axis=1).astype(BF16) for n in thirds]
     table_at = lax.broadcasted_iota(jnp.int32, (slots, table_ref.shape[1]), 1).astype(F32)
-    slot_gate = jnp.sum(jnp.where(table_at == slot_entry, table_ref[...], 0.0), axis=1, keepdims=True)
-
+
+    def gate_of(n):
+        at = jnp.sum((select + spill[n]) * entry, axis=1, keepdims=True)
+        return jnp.sum(jnp.where(table_at == at, table_ref[...], 0.0), axis=1, keepdims=True)
+
+    def picked(n, source):
+        both = jnp.concatenate([source[:, tail * n : tail * (n + 1)], source[:, packed:]], axis=0)
+        return jnp.dot(pickers[n], both, preferred_element_type=F32)
+
+    gates = [gate_of(n) for n in thirds]
     loads[0].wait()
-    picked_x = jnp.dot(picker, tok[...], preferred_element_type=F32)
     loads[1].wait()
-    picked_cot = slot_gate * jnp.dot(picker, cot[...], preferred_element_type=F32)
-
-    def block(k):
-        at = slice(k * SLOT_ROWS, (k + 1) * SLOT_ROWS)
-        return jnp.concatenate([picked_x[at], picked_cot[at]], axis=0).astype(BF16)
-
-    for k in range(1, DEPTH):
-        sbuf[k - 1] = block(k)
-    rows[0, 0, 0] = block(0)
+    for n in thirds:
+        cols = slice(tail * n, tail * (n + 1))
+        from_x = picked(n, tok)
+        from_cot = gates[n] * picked(n, cot)
+        for k in ks_all:
+            at = slice(k * SLOT_ROWS, (k + 1) * SLOT_ROWS)
+            block = jnp.concatenate([from_x[at], from_cot[at]], axis=0).astype(BF16)
+            if k == 0:
+                rows[0, 0, 0, :, cols] = block
+            else:
+                sbuf[k - 1, :, cols] = block
     pl.semaphore_wait(barrier, 6)
 
     def spread(k):
@@ -237,11 +261,9 @@
         c_rx[k].start()
         c_p[2][k].start()
 
-    for k in (3, 1, 2):
+    for k in (1, 3, 2):
         c_z[k].start()
     spread(0)
-    for load in loads[2:]:
-        load.wait()
     c_z[1].wait_recv()
     spread(1)
     relay(0)
@@ -253,26 +275,57 @@
     relay(2)
     relay(3)
 
+    def spill_map(size, transposed):
+        to = lax.broadcasted_iota(jnp.int32, (size, size), 1 if transposed else 0)
+        at = lax.broadcasted_iota(jnp.int32, (size, size), 0 if transposed else 1)
+        same = lax.shift_right_logical(to, 3) == lax.shift_right_logical(at, 3)
+        to, at = to & 7, at & 7
+        return [
+            jnp.where(same & (at >= SLOTS) & (to == 3 * (at - SLOTS) + n), 1.0, 0.0).astype(BF16)
+            for n in thirds
+        ]
+
+    unspill = spill_map(2 * DEPTH * BLOCK, False)
+    respill = spill_map(2 * slots, True)
+    held = (lax.broadcasted_iota(jnp.int32, (2 * slots, 1), 0) & 7) < SLOTS
+    for load in loads[2:]:
+        load.wait()
+    across = (((1,), (1,)), ((), ()))
+
     def piece(q):
         for k in ks_all:
             c_p[q][k].wait_recv()
-        pre = lax.dot_general(
-            rows[q].reshape(2 * DEPTH * BLOCK, width), w[...],
-            (((1,), (1,)), ((), ())), preferred_element_type=F32,
-        ).reshape(2 * DEPTH, BLOCK, 3 * units)
+        size = 2 * DEPTH * BLOCK
+        landed = rows[q].reshape(size, packed)
+        ends = jnp.zeros((size, tail), F32)
+        for n in thirds:
+            ends = ends + jnp.dot(
+                unspill[n], landed[:, tail * n : tail * (n + 1)], preferred_element_type=F32
+            )
+        ends = ends.astype(BF16)
+        tails[q * size : (q + 1) * size] = ends
+        pre = lax.dot_general(landed, w[:, :packed], across, preferred_element_type=F32)
+        pre = pre + lax.dot_general(ends, w[:, packed:], across, preferred_element_type=F32)
+        pre = pre.reshape(2 * DEPTH, BLOCK, 3 * units)
         pre_x = pre[:, :SLOT_ROWS].reshape(2 * slots, 3 * units)
         pre_c = pre[:, SLOT_ROWS:].reshape(2 * slots, 3 * units)
         gate, up, hidden_delta = pre_x[:, :units], pre_x[:, units : 2 * units], pre_c[:, 2 * units :]
         sig = jax.nn.sigmoid(gate)
         active = gate * sig
-        hidden = active * up
+        hidden = jnp.where(held, active * up, 0.0)
         gate_delta = hidden_delta * up * (sig * (1.0 + gate * (1.0 - sig)))
-        up_delta = hidden_delta * active
-        both = jnp.concatenate([gate_delta, up_delta], axis=1)
-        back = jnp.dot(both.astype(BF16), w[: 2 * units], preferred_element_type=F32)
-        pa_s[q] = back[slots:].astype(BF16)
+        gate_delta = jnp.where(held, gate_delta, 0.0)
+        up_delta = jnp.where(held, hidden_delta * active, 0.0)
+        both = jnp.concatenate([gate_delta, up_delta], axis=1).astype(BF16)
+        for n in thirds:
+            cols = slice(tail * n, tail * (n + 1))
+            moved = jnp.dot(respill[n], both, preferred_element_type=F32).astype(BF16)
+            left = jnp.concatenate([both, moved], axis=1)
+            right = jnp.concatenate([w[: 2 * units, cols], w[: 2 * units, packed:]], axis=0)
+            back = jnp.dot(left, right, preferred_element_type=F32)
+            pa_s[q, :, cols] = back[slots:].astype(BF16)
+            acc[q, :, cols] = back[:slots]
         c_pa[q].start()
-        acc[q] = back[:slots]
         none = jnp.zeros((2 * DEPTH, SLOT_ROWS, units), F32)
 
         def placed(values, first):
@@ -294,17 +347,17 @@
     piece(2)
     piece(3)
 
-    chunks = wgrad_out.shape[1] // 512
+    chunks = 4
     stores = [
         pltpu.make_async_copy(
-            wgrad.at[:, pl.ds(512 * n, 512)], wgrad_out.at[:, pl.ds(512 * n, 512)], out_sem.at[n]
+            wgrad.at[:, pl.ds(tail * n, tail)], wgrad_out.at[:, pl.ds(tail * n, tail)], out_sem.at[n]
         )
         for n in range(chunks)
     ]
 
     def weights(n):
-        at = slice(512 * n, 512 * (n + 1))
-        right = rows[:, :, :, :, at].reshape(PLANE * 2 * DEPTH * BLOCK, 512)
+        at = slice(tail * n, tail * (n + 1))
+        right = rows[:, :, :, :, at].reshape(tails.shape) if n < 3 else tails[...]
         wgrad[:, at] = lax.dot_general(
             delta[...], right, (((0,), (0,)), ((), ())), preferred_element_type=F32
         ).astype(BF16)
@@ -315,45 +368,57 @@
         return acc[q] + pa_r[q].astype(F32)
 
     one = merged(1)
-    bx_s[0] = one[:, :half].astype(BF16)
+    bx_s[0] = one[:, :cut].astype(BF16)
     c_bx[0].start()
     acc[1] = one
     two = merged(2)
-    by_s[0] = two[:, half:].astype(BF16)
+    by_s[0] = two[:, cut:].astype(BF16)
     c_by[0].start()
     acc[2] = two
     three = merged(3)
-    bx_s[1] = three[:, :half].astype(BF16)
+    bx_s[1] = three[:, :cut].astype(BF16)
     c_bx[1].start()
-    by_s[1] = three[:, half:].astype(BF16)
+    by_s[1] = three[:, cut:].astype(BF16)
     c_by[1].start()
     acc[0] = merged(0)
     for n in range(0, chunks - 2):
         weights(n)
     c_bx[1].wait_recv()
-    cy_s[...] = (acc[2, :, :half] + bx_r[1].astype(F32)).astype(BF16)
+    cy_s[...] = (acc[2, :, :cut] + bx_r[1].astype(F32)).astype(BF16)
     c_cy.start()
     c_by[1].wait_recv()
-    cx_s[...] = (acc[1, :, half:] + by_r[1].astype(F32)).astype(BF16)
+    cx_s[...] = (acc[1, :, cut:] + by_r[1].astype(F32)).astype(BF16)
     c_cx.start()
     weights(chunks - 2)
     c_bx[0].wait_recv()
     c_by[0].wait_recv()
     c_cy.wait_recv()
     c_cx.wait_recv()
-    left = acc[0, :, :half] + bx_r[0].astype(F32) + cy_r[...].astype(F32)
-    right = acc[0, :, half:] + by_r[0].astype(F32) + cx_r[...].astype(F32)
-    for k in (3, 1, 2):
+    left = acc[0, :, :cut] + bx_r[0].astype(F32) + cy_r[...].astype(F32)
+    right = acc[0, :, cut:] + by_r[0].astype(F32) + cx_r[...].astype(F32)
+    filler = jnp.zeros((SLOT_ROWS, 2 * cut - packed), F32)
+    for k in (3, 2, 1):
         at = slice(k * SLOT_ROWS, (k + 1) * SLOT_ROWS)
-        zs_s[k - 1] = jnp.concatenate([left[at], right[at]], axis=0).astype(BF16)
+        zs_s[k - 1] = jnp.concatenate([left[at], jnp.concatenate([right[at], filler], axis=1)], axis=0).astype(BF16)
         c_zs[k].start()
     weights(chunks - 1)
     parts = [jnp.concatenate([left[:SLOT_ROWS], right[:SLOT_ROWS]], axis=1)]
     for k in range(1, DEPTH):
         c_zs[k].wait_recv()
         got = zs_r[k - 1].astype(F32)
-        parts.append(jnp.concatenate([got[:SLOT_ROWS], got[SLOT_ROWS:]], axis=1))
-    ps_out[...] = jnp.concatenate(parts, axis=0).astype(BF16)
+        parts.append(jnp.concatenate([got[:SLOT_ROWS], got[SLOT_ROWS:, : packed - cut]], axis=1))
+    slot_grads = jnp.concatenate(parts, axis=0).astype(BF16)
+    down = (((0,), (0,)), ((), ()))
+    tokens_out[:, :packed] = lax.dot_general(
+        select.astype(BF16), slot_grads, down, preferred_element_type=F32
+    ).astype(BF16)
+    rest = jnp.zeros((count, tail), F32)
+    for n in thirds:
+        rest = rest + lax.dot_general(
+            spill[n].astype(BF16), slot_grads[:, tail * n : tail * (n + 1)], down,
+            preferred_element_type=F32,
+        )
+    tokens_out[:, packed:] = rest.astype(BF16)
 
     for copy in c_z[1:] + c_x + c_y + c_rx + c_ry + sum(c_p, []) + c_pa + c_bx + c_by:
         copy.wait_send()
@@ -366,47 +431,50 @@
 def per_device_fast(tokens, cotangent, route, gate_index, gate_table, w_gate, w_up, w_down):
     count, width = tokens.shape
     units = w_gate.shape[0]
-    half = width // 2
+    packed = width // 4 * 3
+    cut = (packed // 128 + 1) // 2 * 128
     slots = DEPTH * SLOT_ROWS
     vmem = pl.BlockSpec(memory_space=pltpu.VMEM)
     hbm = pl.BlockSpec(memory_space=pltpu.HBM)
-    slot_grads, select, weight_grads = pl.pallas_call(
+    grad_tokens, weight_grads = pl.pallas_call(
         kernel,
         out_shape=(
-            jax.ShapeDtypeStruct((slots, width), BF16),
-            jax.ShapeDtypeStruct((count, 128), BF16),
+            jax.ShapeDtypeStruct((count, width), BF16),
             jax.ShapeDtypeStruct((3 * units, width), BF16),
         ),
-        in_specs=[vmem] * 3 + [hbm] * 5,
-        out_specs=(vmem, vmem, pl.BlockSpec(memory_space=pl.ANY)),
+        in_specs=[hbm] * 8,
+        out_specs=(vmem, pl.BlockSpec(memory_space=pl.ANY)),
         scratch_shapes=[
+            pltpu.VMEM(route.shape[::-1], jnp.int32),
+            pltpu.VMEM(route.shape[::-1], jnp.int32),
+            pltpu.VMEM((1, gate_table.shape[0]), F32),
             pltpu.VMEM((count, width), BF16),
             pltpu.VMEM((count, width), BF16),
             pltpu.VMEM((3 * units, width), BF16),
-            pltpu.VMEM((DEPTH - 1, BLOCK, width), BF16),
-            pltpu.VMEM((PLANE, 2, DEPTH, BLOCK, width), BF16),
+            pltpu.VMEM((DEPTH - 1, BLOCK, packed), BF16),
+            pltpu.VMEM((PLANE, 2, DEPTH, BLOCK, packed), BF16),
+            pltpu.VMEM((PLANE * 2 * DEPTH * BLOCK, width - packed), BF16),
             pltpu.VMEM((PLANE * 2 * DEPTH * BLOCK, 3 * units), BF16),
-            pltpu.VMEM((PLANE, slots, width), F32),
-            pltpu.VMEM((PLANE, slots, width), BF16),
-            pltpu.VMEM((PLANE, slots, width), BF16),
+            pltpu.VMEM((PLANE, slots, packed), F32),
+            pltpu.VMEM((PLANE, slots, packed), BF16),
+            pltpu.VMEM((PLANE, slots, packed), BF16),
         ]
-        + [pltpu.VMEM((2, slots, half), BF16)] * 4
-        + [pltpu.VMEM((slots, half), BF16)] * 4
-        + [pltpu.VMEM((DEPTH - 1, BLOCK, half), BF16)] * 2
+        + [pltpu.VMEM((2, slots, cut), BF16)] * 2
+        + [pltpu.VMEM((2, slots, packed - cut), BF16)] * 2
+        + [pltpu.VMEM((slots, packed - cut), BF16)] * 2
+        + [pltpu.VMEM((slots, cut), BF16)] * 2
+        + [pltpu.VMEM((DEPTH - 1, BLOCK, cut), BF16)] * 2
         + [
             pltpu.VMEM((3 * units, width), BF16),
-            pltpu.SemaphoreType.DMA((5,)),
-            pltpu.SemaphoreType.DMA((width // 512,)),
+            pltpu.SemaphoreType.DMA((8,)),
+            pltpu.SemaphoreType.DMA((4,)),
             pltpu.SemaphoreType.DMA((52,)),
             pltpu.SemaphoreType.DMA((52,)),
         ],
         compiler_params=pltpu.CompilerParams(
-            collective_id=0, has_side_effects=True, vmem_limit_bytes=40 * 1024 * 1024
+            collective_id=0, has_side_effects=True, vmem_limit_bytes=VMEM_BYTES
         ),
-    )(route, gate_index, gate_table.reshape(1, -1), tokens, cotangent, w_gate, w_up, w_down)
-    grad_tokens = jnp.dot(
-        select[:, :slots], slot_grads, preferred_element_type=jnp.float32
-    ).astype(jnp.bfloat16)
+    )(route.T, gate_index.T, gate_table.reshape(1, -1), tokens, cotangent, w_gate, w_up, w_down)
     wide = weight_grads.astype(jnp.float32)
     return (grad_tokens, wide[:units], wide[units : 2 * units], wide[2 * units :])
 

time: 55.1 us -> 45.5 us (0.83)
  local copies, waits for them, and re-layouts: 9.75 us -> 4.44 us
  Pallas kernels: 43.2 us -> 40.2 us
  matrix products: 1.14 us -> 0 us
    unnamed x14 -> x3, local copies, waits for them, and re-layouts: 7.69 us -> 0.84 us
    pallas_call x1, Pallas kernels: 43.2 us -> 40.2 us  [per_device_fast(): pl.pallas_call(kernel, out_shape=(jax.ShapeDtypeStruct((count, width), BF...]
    slice x1, local copies, waits for them, and re-layouts: 2.05 us -> 3.6 us  [per_device_fast(): return (grad_tokens, wide[:units], wide[units:2 * units], wide[2 * units:])]
    dot_general x1 -> x0, matrix products: 1.14 us -> none  [per_device_fast(): jnp.dot(select[:, :slots], slot_grads, preferred_element_type=jnp.float32)]
where the time goes in v2:
time: 45.5 us; the launch traced here: 45.3 us
  Pallas kernels  40.2 us (88%)
  local copies, waits for them, and re-layouts  4.44 us (10%)
  between operations  0.65 us (1%)
    pallas_call x1, Pallas kernels, per_device_fast(): pl.pallas_call(kernel, out_shape=(jax.ShapeDtypeStruct((count, width), BF...  40.2 us
    slice x1, local copies, waits for them, and re-layouts, per_device_fast(): return (grad_tokens, wide[:units], wide[units:2 * units], wide[2 * units:])  3.6 us

profile of v2, /device:TPU:0, one launch (start us, length us, event | category | flops | bytes accessed | tf_op | source)
XLA Modules:
  0.0 45.3 jit_solution(17376095617247478714)
XLA Ops:
  0.6 40.2 %shard_map.111 = (bf16[128,2560]{1,0:T(8,128)(2,1)}, bf16[384,2560]{1,0:T(8,128)(2,1)}) custom-call(s32[6,128]{1,0:T(8,128)} %bitcast.3, s32[6,128]{1,0:T(8,128)} %bitcast.4, f32[1,256]{1,0:T(1,128)} %bitcast.5, bf16[128,2560]{1,0:T(8,128)(2,1)} %tok_hbm.1, bf16[128,2560]{1,0:T(8,128)(2,1)} %cot_hbm.1, bf16[128,2560]{1,0:T(8,128)(2,1)} %wg_hbm.1, ...), custom_call_target="tpu_custom_call" | custom-call | tf_op jit(solution)/shard_map/pallas_call | solution.py:439
  40.9 0.0 copy-start
  40.9 3.6 %fusion = (f32[128,2560]{1,0:T(8,128)}, f32[128,2560]{1,0:T(8,128)}, f32[128,2560]{1,0:T(8,128)}) fusion(bf16[384,2560]{1,0:T(8,128)(2,1)} %get-tuple-element.7), kind=kLoop, calls=%fused_computation | loop fusion | bytes 7864320 | tf_op jit(solution)/shard_map/slice | solution.py:479
  44.5 0.0 copy-done
  44.5 0.8 %copy.13 = bf16[128,2560]{1,0:T(8,128)(2,1)} copy(bf16[128,2560]{1,0:T(8,128)(2,1)S(1)} %copy-done) | data formatting | bytes 1310720
Async XLA Ops:
  40.9 3.6 %copy-start = (bf16[128,2560]{1,0:T(8,128)(2,1)S(1)}, bf16[128,2560]{1,0:T(8,128)(2,1)}, u32[]{:S(2)}) copy-start(bf16[128,2560]{1,0:T(8,128)(2,1)} %get-tuple-element.15) | copy-start | bytes 1966084

commit v3 on v2

--- a/solution.py
+++ b/solution.py
@@ -345,23 +345,6 @@
         c_p[3][k].start()
     piece(1)
     piece(2)
-    piece(3)
-
-    chunks = 4
-    stores = [
-        pltpu.make_async_copy(
-            wgrad.at[:, pl.ds(tail * n, tail)], wgrad_out.at[:, pl.ds(tail * n, tail)], out_sem.at[n]
-        )
-        for n in range(chunks)
-    ]
-
-    def weights(n):
-        at = slice(tail * n, tail * (n + 1))
-        right = rows[:, :, :, :, at].reshape(tails.shape) if n < 3 else tails[...]
-        wgrad[:, at] = lax.dot_general(
-            delta[...], right, (((0,), (0,)), ((), ())), preferred_element_type=F32
-        ).astype(BF16)
-        stores[n].start()
 
     def merged(q):
         c_pa[q].wait_recv()
@@ -375,6 +358,24 @@
     by_s[0] = two[:, cut:].astype(BF16)
     c_by[0].start()
     acc[2] = two
+    piece(3)
+
+    chunks = 4
+    stores = [
+        pltpu.make_async_copy(
+            wgrad.at[:, pl.ds(tail * n, tail)], wgrad_out.at[:, pl.ds(tail * n, tail)], out_sem.at[n]
+        )
+        for n in range(chunks)
+    ]
+
+    def weights(n):
+        at = slice(tail * n, tail * (n + 1))
+        right = rows[:, :, :, :, at].reshape(tails.shape) if n < 3 else tails[...]
+        wgrad[:, at] = lax.dot_general(
+            delta[...], right, (((0,), (0,)), ((), ())), preferred_element_type=F32
+        ).astype(BF16)
+        stores[n].start()
+
     three = merged(3)
     bx_s[1] = three[:, :cut].astype(BF16)
     c_bx[1].start()

time: 45.5 us -> 46.1 us (1.013)
  Pallas kernels: 40.2 us -> 40.8 us
    pallas_call x1, Pallas kernels: 40.2 us -> 40.8 us  [per_device_fast(): pl.pallas_call(kernel, out_shape=(jax.ShapeDtypeStruct((count, width), BF...]
where the time goes in v3:
time: 46.1 us; the launch traced here: 45.9 us
  Pallas kernels  40.8 us (89%)
  local copies, waits for them, and re-layouts  4.44 us (10%)
  between operations  0.65 us (1%)
    pallas_call x1, Pallas kernels, per_device_fast(): pl.pallas_call(kernel, out_shape=(jax.ShapeDtypeStruct((count, width), BF...  40.8 us
    slice x1, local copies, waits for them, and re-layouts, per_device_fast(): return (grad_tokens, wide[:units], wide[units:2 * units], wide[2 * units:])  3.6 us

profile of v3, /device:TPU:0, one launch (start us, length us, event | category | flops | bytes accessed | tf_op | source)
XLA Modules:
  0.0 45.9 jit_solution(4890428234275615291)
XLA Ops:
  0.6 40.8 %shard_map.111 = (bf16[128,2560]{1,0:T(8,128)(2,1)}, bf16[384,2560]{1,0:T(8,128)(2,1)}) custom-call(s32[6,128]{1,0:T(8,128)} %bitcast.3, s32[6,128]{1,0:T(8,128)} %bitcast.4, f32[1,256]{1,0:T(1,128)} %bitcast.5, bf16[128,2560]{1,0:T(8,128)(2,1)} %tok_hbm.1, bf16[128,2560]{1,0:T(8,128)(2,1)} %cot_hbm.1, bf16[128,2560]{1,0:T(8,128)(2,1)} %wg_hbm.1, ...), custom_call_target="tpu_custom_call" | custom-call | tf_op jit(solution)/shard_map/pallas_call | solution.py:440
  41.5 0.0 copy-start
  41.5 3.6 %fusion = (f32[128,2560]{1,0:T(8,128)}, f32[128,2560]{1,0:T(8,128)}, f32[128,2560]{1,0:T(8,128)}) fusion(bf16[384,2560]{1,0:T(8,128)(2,1)} %get-tuple-element.7), kind=kLoop, calls=%fused_computation | loop fusion | bytes 7864320 | tf_op jit(solution)/shard_map/slice | solution.py:480
  45.1 0.0 copy-done
  45.1 0.8 %copy.13 = bf16[128,2560]{1,0:T(8,128)(2,1)} copy(bf16[128,2560]{1,0:T(8,128)(2,1)S(1)} %copy-done) | data formatting | bytes 1310720
Async XLA Ops:
  41.5 3.6 %copy-start = (bf16[128,2560]{1,0:T(8,128)(2,1)S(1)}, bf16[128,2560]{1,0:T(8,128)(2,1)}, u32[]{:S(2)}) copy-start(bf16[128,2560]{1,0:T(8,128)(2,1)} %get-tuple-element.15) | copy-start | bytes 1966084
